TPU v7x, 256 devices: a whole 4x4x8 slice. The times are simulated.
256 devices in a mesh: tgt: 64 (over x, z, core), rep: 4 (over y).
Axes of the slice: x: 4, y: 4, z: 8, core: 2. Of those that a mesh axis runs over, the one named last changes fastest.
Arguments:
- flux: bfloat16 [16384, 7808], P(('tgt', 'rep')), may hold values from 0.19921875 to 4
- ivar: bfloat16 [16384, 7808], P(('tgt', 'rep')), may hold values from 0.099609375 to 10
- row_target: int32 [16384], P(('tgt', 'rep')), may hold values from 0 to 8191, as said below
- start_w: float32 [8192, 64], P(('tgt', 'rep')), may hold values from 0.02 to 0.25
- start_h: float32 [64, 7808], P(None, 'tgt'), may hold values from 0.02 to 0.25
Outputs:
- activations: float32 [8192, 64], P(('tgt', 'rep'))
- templates: float32 [64, 7808], P(None, 'tgt')
Inputs may be any that keep to these rules, and one draw needn't show every extreme that they name: `row_target`: row i lies on device d = i // 64; its target t is owned by device t // 32, which has the same index along rep as d, i.e. (t // 32) % 4 == d % 4. The rows of one device name targets of one owning device at most 2 times, and every device reaches 2 for some owner. A target may have several rows or none.
All inputs are finite; a program needn't handle non-finite values.
Results may differ from a plain program's by a relative error of at most 0.035.
Values may be sent and summed in bfloat16 or wider, within the bound.
No kernel may reach another device: no remote copies, remote signals or barrier semaphores. Data moves between devices by JAX's collectives and lax.ppermute only.
A program may use at most 64 MiB of HBM per device.

v0:
```python
import jax
import jax.numpy as jnp
from jax import lax
from jax.sharding import PartitionSpec as P

SWEEPS = 2
PRIOR_IVAR = 0.5
EPSILON = 1e-06


def update_columns(activation, cross, gram):

    def column_step(index, current):
        gram_col = lax.dynamic_index_in_dim(gram, index, 1, keepdims=False)
        pivot = lax.dynamic_index_in_dim(gram_col, index, 0, keepdims=False)
        column = lax.dynamic_index_in_dim(current, index, 1, keepdims=False)
        wanted = lax.dynamic_index_in_dim(cross, index, 1, keepdims=False)
        fitted = jnp.dot(current, gram_col, precision=lax.Precision.HIGHEST)
        updated = jnp.maximum(column + (wanted - fitted) / (pivot + EPSILON), 0.0)
        return lax.dynamic_update_index_in_dim(current, updated, index, 1)

    return lax.fori_loop(0, activation.shape[1], column_step, activation)


def update_rows(templates, proj, gram):

    def row_step(index, current):
        gram_row = lax.dynamic_index_in_dim(gram, index, 0, keepdims=False)
        pivot = lax.dynamic_index_in_dim(gram_row, index, 0, keepdims=False)
        row_now = lax.dynamic_index_in_dim(current, index, 0, keepdims=False)
        wanted = lax.dynamic_index_in_dim(proj, index, 0, keepdims=False)
        fitted = jnp.dot(gram_row, current, precision=lax.Precision.HIGHEST)
        updated = jnp.maximum(row_now + (wanted - fitted) / (pivot + EPSILON), 0.0)
        return lax.dynamic_update_index_in_dim(current, updated, index, 0)

    return lax.fori_loop(0, templates.shape[0], row_step, templates)


def shards(flux, ivar, row_target, start_w, start_h):
    tgt_count = lax.axis_size("tgt")
    rep_count = lax.axis_size("rep")
    rows_dev = flux.shape[0]
    tgt_dev = start_w.shape[0]
    weighted = (ivar.astype(jnp.float32) * flux.astype(jnp.float32)).astype(jnp.bfloat16)
    owner_dev = row_target // tgt_dev
    peer_dev = owner_dev // rep_count
    capacity = 2 * rows_dev // tgt_count
    peer_onehot = (peer_dev[:, None] == jnp.arange(tgt_count, dtype=jnp.int32)[None, :]).astype(
        jnp.int32
    )
    running = jnp.cumsum(peer_onehot, axis=0)
    slot_index = jnp.sum(running * peer_onehot, axis=1) - 1
    place = peer_dev * capacity + slot_index
    source_row = (
        jnp.zeros((tgt_count * capacity,), jnp.int32)
        .at[place]
        .set(jnp.arange(rows_dev, dtype=jnp.int32))
    )
    filled = jnp.zeros((tgt_count * capacity,), jnp.int32).at[place].set(1)
    keep_rows = filled[:, None].astype(jnp.bfloat16)
    send_weighted = jnp.take(weighted, source_row, axis=0) * keep_rows
    send_ivar = jnp.take(ivar, source_row, axis=0) * keep_rows
    send_target = jnp.where(filled == 1, jnp.take(row_target, source_row, axis=0), -1)
    got_weighted, got_ivar, got_target = (
        lax.all_to_all(send_weighted, "tgt", split_axis=0, concat_axis=0, tiled=True),
        lax.all_to_all(send_ivar, "tgt", split_axis=0, concat_axis=0, tiled=True),
        lax.all_to_all(send_target, "tgt", split_axis=0, concat_axis=0, tiled=True),
    )
    first_target = (lax.axis_index("tgt") * rep_count + lax.axis_index("rep")) * tgt_dev
    selector = (
        got_target[None, :] - first_target == jnp.arange(tgt_dev, dtype=jnp.int32)[:, None]
    ).astype(jnp.bfloat16)
    numerator = jnp.dot(selector, got_weighted, preferred_element_type=jnp.float32)
    denominator = jnp.dot(selector, got_ivar, preferred_element_type=jnp.float32)
    coadd = (numerator / (denominator + PRIOR_IVAR)).astype(jnp.bfloat16)
    spectra = lax.all_to_all(coadd, "tgt", split_axis=1, concat_axis=0, tiled=True)
    activation = lax.all_gather(start_w, "tgt", axis=0, tiled=True)
    templates = start_h
    for sweep in range(SWEEPS):
        templ_bf = templates.astype(jnp.bfloat16)
        hgram_part = jnp.dot(templates, templates.T, precision=lax.Precision.HIGHEST)
        cross_part = jnp.dot(spectra, templ_bf.T, preferred_element_type=jnp.float32)
        cross, hgram = lax.psum((cross_part, hgram_part), "tgt")
        activation = update_columns(activation, cross, hgram)
        proj_part = lax.dot_general(
            activation.astype(jnp.bfloat16),
            spectra,
            (((0,), (0,)), ((), ())),
            preferred_element_type=jnp.float32,
        )
        wgram_part = jnp.dot(activation.T, activation, precision=lax.Precision.HIGHEST)
        proj, wgram = lax.psum((proj_part, wgram_part), "rep")
        templates = update_rows(templates, proj, wgram)
    own_w = lax.dynamic_slice_in_dim(activation, lax.axis_index("tgt") * tgt_dev, tgt_dev, 0)
    return (own_w, templates)


def solution(mesh):
    placed = (
        P(("tgt", "rep"), None),
        P(("tgt", "rep"), None),
        P(("tgt", "rep")),
        P(("tgt", "rep"), None),
        P(None, "tgt"),
    )
    return jax.shard_map(
        shards,
        mesh=mesh,
        in_specs=placed,
        out_specs=(P(("tgt", "rep"), None), P(None, "tgt")),
        check_vma=False,
    )
```

profile of v0, /device:TPU:8, one launch (start us, length us, event | category | flops | bytes accessed | tf_op | source)
XLA Modules:
  0.0 1318.5 jit_solution(9789575537605206230)
XLA Ops:
  10.4 1.6 gather_fusion
  13.6 11.9 all-to-all-start
  25.6 6.4 gather_fusion.2
  32.2 3.1 gather_fusion.1
  35.3 4.0 select_multiply_fusion.1
  39.4 1.7 all_to_all.41
  41.1 10.3 all-to-all-start.2
  51.4 5.0 all_to_all.38
  56.4 44.1 %all-to-all-done.2 = bf16[64,2,7808]{2,1,0:T(2,128)(2,1)S(1)} async-done(((bf16[64,2,7808]{2,1,0:T(2,128)(2,1)}), bf16[64,2,7808]{2,1,0:T(2,128)(2,1)S(1)}, u32[]{:S(2)}, u32[]{:S(2)}) %all-to-all-start.2) | async-done | bytes 1998880 | tf_op jit(solution)/shard_map/all_to_all | solution.py:66
  100.5 6.3 all-to-all-start.1
  107.1 4.3 all_to_all.43
  111.7 43.9 %all-to-all-done.1 = bf16[64,2,7808]{2,1,0:T(2,128)(2,1)} async-done(((bf16[64,2,7808]{2,1,0:T(2,128)(2,1)}), bf16[64,2,7808]{2,1,0:T(2,128)(2,1)}, u32[]{:S(2)}, u32[]{:S(2)}) %all-to-all-start.1) | async-done | bytes 1998880 | tf_op jit(solution)/shard_map/all_to_all | solution.py:65
  155.6 4.3 all_to_all.40
  160.3 2.1 all_to_all.44
  162.5 1.1 copy.17
  163.6 5.9 all-to-all-start.3
  169.5 17.1 %all-to-all-done.3 = bf16[32,64,122]{2,0,1:T(8,128)(2,1)S(1)} async-done(((bf16[32,64,122]{2,0,1:T(8,128)(2,1)}), bf16[32,64,122]{2,0,1:T(8,128)(2,1)S(1)}, u32[]{:S(2)}, u32[]{:S(2)}) %all-to-all-start.3) | async-done | bytes 499744 | tf_op jit(solution)/shard_map/all_to_all | solution.py:76
  186.7 1.1 fusion.28
  188.0 247.9 %psum.57 = f32[64,64]{1,0:T(8,128)S(1)} all-reduce(f32[64,64]{1,0:T(8,128)S(1)} %fusion.36), channel_id=1, replica_groups=mesh['tgt'=64,'rep'=4] {'tgt'}, use_global_device_ids=true, to_apply=%region_0.1 | all-reduce | flops 4096 | bytes 32768 | tf_op jit(solution)/shard_map/psum | solution.py:83
  436.0 47.2 %all_gather.3 = f32[2048,64]{1,0:T(8,128)S(1)} all-gather(f32[32,64]{1,0:T(8,128)S(1)} %copy-done.4), channel_id=1, replica_groups=mesh['tgt'=64,'rep'=4] {'tgt'}, dimensions={0}, use_global_device_ids=true | all-gather | bytes 532480 | tf_op jit(solution)/shard_map/all_gather | solution.py:77
  483.5 181.6 %while.64 = (s32[]{:T(128)}, f32[2048,64]{0,1:T(8,128)S(1)}, f32[2048,64]{0,1:T(8,128)}, f32[64,64]{0,1:T(8,128)S(1)}, s32[]{:T(128)}, /*index=5*/s32[]{:T(128)}, s32[]{:T(128)}, f32[1,1]{0,1:T(1,128)}) while((s32[]{:T(128)}, f32[2048,64]{0,1:T(8,128)S(1)}, f32[2048,64]{0,1:T(8,128)}, f32[64,64]{0,1:T(8,128)S(1)}, s32[]{:T(128)}, ...), condition=%wide.region_7.9_spmd, body=%wide.region_6.8_spmd.sunk | while | flops 1581060 | bytes 615053 | solution.py:22
  483.5 0.9 constant_dynamic-slice_fusion.20
  486.4 0.9 constant_dynamic-slice_fusion.20
  497.7 0.9 constant_dynamic-slice_fusion.20
  500.6 0.9 constant_dynamic-slice_fusion.20
  503.4 0.9 constant_dynamic-slice_fusion.20
  506.2 0.9 constant_dynamic-slice_fusion.20
  509.1 0.9 constant_dynamic-slice_fusion.20
  511.9 0.9 constant_dynamic-slice_fusion.20
  514.8 0.9 constant_dynamic-slice_fusion.20
  523.3 0.9 constant_dynamic-slice_fusion.20
  526.1 0.9 constant_dynamic-slice_fusion.20
  528.9 0.9 constant_dynamic-slice_fusion.20
  531.8 0.9 constant_dynamic-slice_fusion.20
  534.6 0.9 constant_dynamic-slice_fusion.20
  537.4 0.9 constant_dynamic-slice_fusion.20
  540.3 0.9 constant_dynamic-slice_fusion.20
  551.6 0.9 constant_dynamic-slice_fusion.20
  554.5 0.9 constant_dynamic-slice_fusion.20
  560.1 0.9 constant_dynamic-slice_fusion.20
  565.8 0.9 constant_dynamic-slice_fusion.20
  568.7 0.9 constant_dynamic-slice_fusion.20
  571.5 0.9 constant_dynamic-slice_fusion.20
  574.3 0.9 constant_dynamic-slice_fusion.20
  577.2 0.9 constant_dynamic-slice_fusion.20
  580.0 0.9 constant_dynamic-slice_fusion.20
  591.3 0.9 constant_dynamic-slice_fusion.20
  594.2 0.9 constant_dynamic-slice_fusion.20
  597.0 0.9 constant_dynamic-slice_fusion.20
  599.9 0.9 constant_dynamic-slice_fusion.20
  602.7 0.9 constant_dynamic-slice_fusion.20
  605.5 0.9 constant_dynamic-slice_fusion.20
  608.4 0.9 constant_dynamic-slice_fusion.20
  616.9 0.9 constant_dynamic-slice_fusion.20
  619.7 0.9 constant_dynamic-slice_fusion.20
  622.6 0.9 constant_dynamic-slice_fusion.20
  625.4 0.9 constant_dynamic-slice_fusion.20
  665.9 14.8 %all-reduce.1 = (f32[64,122]{1,0:T(8,128)S(1)}, f32[64,64]{1,0:T(8,128)S(1)}) all-reduce(f32[64,122]{1,0:T(8,128)S(1)} %fusion.23, f32[64,64]{1,0:T(8,128)S(1)} %fusion.37), channel_id=1, replica_groups=mesh['tgt'=64,'rep'=4] {'rep'}, use_global_device_ids=true, to_apply=%region_9.11 | all-reduce | flops 11904 | bytes 95232 | tf_op jit(solution)/shard_map/psum | solution.py:92
  680.7 91.4 %while.65 = (s32[]{:T(128)}, f32[64,122]{1,0:T(8,128)S(1)}, f32[64,122]{1,0:T(8,128)S(1)}, f32[64,64]{1,0:T(8,128)S(1)}, s32[]{:T(128)}, /*index=5*/s32[]{:T(128)}, s32[]{:T(128)}, f32[1,1]{1,0:T(1,128)}) while((s32[]{:T(128)}, f32[64,122]{1,0:T(8,128)S(1)}, f32[64,122]{1,0:T(8,128)S(1)}, f32[64,64]{1,0:T(8,128)S(1)}, s32[]{:T(128)}, ...), condition=%wide.region_11.13_spmd, body=%wide.region_10.12_spmd.sunk | while | flops 94188 | bytes 37433 | solution.py:36
  772.2 1.1 fusion.26
  773.5 246.2 %psum.61 = f32[64,64]{1,0:T(8,128)S(1)} all-reduce(f32[64,64]{1,0:T(8,128)S(1)} %fusion.38), channel_id=1, replica_groups=mesh['tgt'=64,'rep'=4] {'tgt'}, use_global_device_ids=true, to_apply=%region_12.14 | all-reduce | flops 4096 | bytes 32768 | tf_op jit(solution)/shard_map/psum | solution.py:83
  1019.7 181.6 %while.66 = (s32[]{:T(128)}, f32[2048,64]{0,1:T(8,128)S(1)}, f32[2048,64]{0,1:T(8,128)}, f32[64,64]{0,1:T(8,128)S(1)}, s32[]{:T(128)}, /*index=5*/s32[]{:T(128)}, s32[]{:T(128)}, f32[1,1]{0,1:T(1,128)}) while((s32[]{:T(128)}, f32[2048,64]{0,1:T(8,128)S(1)}, f32[2048,64]{0,1:T(8,128)}, f32[64,64]{0,1:T(8,128)S(1)}, s32[]{:T(128)}, ...), condition=%wide.region_15.17_spmd, body=%wide.region_14.16_spmd.sunk | while | flops 1581060 | bytes 615053 | solution.py:22
  1202.4 17.2 %all-reduce = (f32[64,122]{1,0:T(8,128)S(1)}, f32[64,64]{1,0:T(8,128)S(1)}) all-reduce(f32[64,122]{1,0:T(8,128)S(1)} %fusion.21, f32[64,64]{1,0:T(8,128)S(1)} %fusion.39), channel_id=1, replica_groups=mesh['tgt'=64,'rep'=4] {'rep'}, use_global_device_ids=true, to_apply=%region_17.19 | all-reduce | flops 11904 | bytes 95232 | tf_op jit(solution)/shard_map/psum | solution.py:92
  1219.7 91.4 %while.67 = (s32[]{:T(128)}, f32[64,122]{1,0:T(8,128)S(1)}, f32[64,122]{1,0:T(8,128)S(1)}, f32[64,64]{1,0:T(8,128)S(1)}, s32[]{:T(128)}, /*index=5*/s32[]{:T(128)}, s32[]{:T(128)}, f32[1,1]{1,0:T(1,128)}) while((s32[]{:T(128)}, f32[64,122]{1,0:T(8,128)S(1)}, f32[64,122]{1,0:T(8,128)S(1)}, f32[64,64]{1,0:T(8,128)S(1)}, s32[]{:T(128)}, ...), condition=%wide.region_19.21_spmd, body=%wide.region_18.20_spmd.sunk | while | flops 94188 | bytes 37433 | solution.py:36
  (1035 shorter events, 345.4 us)
Async XLA Ops:
  13.6 27.5 %all-to-all-start = ((s32[64,2,1]{1,2,0:T(1,128)}), s32[64,2,1]{1,2,0:T(1,128)S(1)}, u32[]{:S(2)}, u32[]{:S(2)}) async-start(s32[64,2,1]{1,2,0:T(1,128)} %bitcast.26), calls=%async_computation | async-start | bytes 65536 | tf_op jit(solution)/shard_map/all_to_all | solution.py:67
  25.5 6.4 copy-start
  25.5 6.4 copy-start.3
  41.1 59.4 %all-to-all-start.2 = ((bf16[64,2,7808]{2,1,0:T(2,128)(2,1)}), bf16[64,2,7808]{2,1,0:T(2,128)(2,1)S(1)}, u32[]{:S(2)}, u32[]{:S(2)}) async-start(bf16[64,2,7808]{2,1,0:T(2,128)(2,1)} %all_to_all.41), calls=%async_computation.2 | async-start | bytes 3997696 | tf_op jit(solution)/shard_map/all_to_all | solution.py:66
  100.5 6.3 copy-start.2
  100.5 55.1 %all-to-all-start.1 = ((bf16[64,2,7808]{2,1,0:T(2,128)(2,1)}), bf16[64,2,7808]{2,1,0:T(2,128)(2,1)}, u32[]{:S(2)}, u32[]{:S(2)}) async-start(bf16[64,2,7808]{2,1,0:T(2,128)(2,1)} %all_to_all.38), calls=%async_computation.1 | async-start | bytes 3997696 | tf_op jit(solution)/shard_map/all_to_all | solution.py:65
  162.4 273.6 %copy-start.4 = (f32[32,64]{1,0:T(8,128)S(1)}, f32[32,64]{1,0:T(8,128)}, u32[]{:S(2)}) copy-start(f32[32,64]{1,0:T(8,128)} %param.18) | copy-start | bytes 24580
  163.6 23.1 %all-to-all-start.3 = ((bf16[32,64,122]{2,0,1:T(8,128)(2,1)}), bf16[32,64,122]{2,0,1:T(8,128)(2,1)S(1)}, u32[]{:S(2)}, u32[]{:S(2)}) async-start(bf16[32,64,122]{2,0,1:T(8,128)(2,1)} %copy.17), calls=%async_computation.3 | async-start | bytes 1048576 | tf_op jit(solution)/shard_map/all_to_all | solution.py:76
  169.5 314.1 %all-reduce.5.cloned.1.call-start = ((), (), s32[]{:S(2)}) async-start(), calls=%async_computation.4 | async-start | bytes 1048576 | tf_op jit(solution)/shard_map/psum | solution.py:83
  187.8 831.9 %all-reduce.7.cloned.1.call-start = ((), (), s32[]{:S(2)}) async-start(), calls=%async_computation.5 | async-start | bytes 1048576 | tf_op jit(solution)/shard_map/psum | solution.py:83
  1311.1 0.6 copy-start.1
Sparse Core Ops, SparseCore 0:
  187.9 178.6 all-reduce.4
  773.4 179.9 all-reduce.6
where the time goes:
time: 1330 us; the launch traced here: 1320 us
  blocking collectives  573 us (43%)
  local copies, waits for them, and re-layouts  335 us (25%)
  loops' own time  179 us (13%)
  waiting for transfers between devices  105 us (8%)
  matrix products  70.2 us (5%)
  starting transfers between devices  34.5 us (3%)
  between operations  14.4 us (1%)
    psum x2, blocking collectives, shards(): cross, hgram = lax.psum((cross_part, hgram_part), 'tgt')  494 us
    dynamic_slice x128, local copies, waits for them, and re-layouts, column_step(): wanted = lax.dynamic_index_in_dim(cross, index, 1, keepdims=False)  110 us
    another operation x2, loops' own time, update_columns(): return lax.fori_loop(0, activation.shape[1], column_step, activation)  93.4 us
    dynamic_slice x128, local copies, waits for them, and re-layouts, column_step(): pivot = lax.dynamic_index_in_dim(gram_col, index, 0, keepdims=False)  85.8 us
    another operation x2, loops' own time, update_rows(): return lax.fori_loop(0, templates.shape[0], row_step, templates)  85.8 us
    dynamic_slice x128, local copies, waits for them, and re-layouts, row_step(): pivot = lax.dynamic_index_in_dim(gram_row, index, 0, keepdims=False)  75.3 us
    all_gather x1, blocking collectives, shards(): activation = lax.all_gather(start_w, 'tgt', axis=0, tiled=True)  47.2 us
    dot_general x128, matrix products, column_step(): fitted = jnp.dot(current, gram_col, precision=lax.Precision.HIGHEST)  46.8 us
  transfers between devices with their start and end apart: 6, of which 3 were waited for; matrix products, arithmetic and copies ran while one was open for 1% of the time, Pallas kernels for 0%

commit v1 on v0

--- a/solution.py
+++ b/solution.py
@@ -1,3 +1,4 @@
+import functools
 import jax
 import jax.numpy as jnp
 from jax import lax
@@ -6,6 +7,39 @@
 SWEEPS = 2
 PRIOR_IVAR = 0.5
 EPSILON = 1e-06
+
+
+def match_thing(in_array, dim_at):
+    in_array = jnp.moveaxis(in_array, 0, dim_at)
+    local_now = in_array.shape
+    clean = in_array.reshape(
+        *local_now[:dim_at], local_now[dim_at] * local_now[dim_at + 1], *local_now[dim_at + 2 :]
+    )
+    return clean
+
+
+def fill_state(target, across):
+    tile_out = target[None]
+    world = lax.axis_size(across)
+    for tick in range(world.bit_length() - 1):
+        reply = 1 << tick
+        f_next = lax.ppermute(
+            tile_out, axis_name=across, perm=[(pp, pp ^ reply) for pp in range(world)]
+        )
+        e_now = jnp.stack([tile_out, f_next])
+        r_now = lax.axis_index(across)
+        y2 = r_now >> tick & 1
+        tile_out = jnp.where(y2 == 0, e_now, e_now[::-1]).reshape(-1, *target.shape)
+    return tile_out
+
+
+def threads_scan(sample, arr, ndim_at):
+    q_next = fill_state(sample, arr)
+    block_next = match_thing(q_next, ndim_at)
+    return block_next
+
+
+counts_see = functools.partial(threads_scan, arr="tgt", ndim_at=0)
 
 
 def update_columns(activation, cross, gram):
@@ -74,7 +108,7 @@
     denominator = jnp.dot(selector, got_ivar, preferred_element_type=jnp.float32)
     coadd = (numerator / (denominator + PRIOR_IVAR)).astype(jnp.bfloat16)
     spectra = lax.all_to_all(coadd, "tgt", split_axis=1, concat_axis=0, tiled=True)
-    activation = lax.all_gather(start_w, "tgt", axis=0, tiled=True)
+    activation = counts_see(start_w)
     templates = start_h
     for sweep in range(SWEEPS):
         templ_bf = templates.astype(jnp.bfloat16)

time: 1330 us -> 1470 us (1.11)
  waiting for transfers between devices: 105 us -> 285 us
  blocking collectives: 573 us -> 526 us
  starting transfers between devices: 34.5 us -> 49.5 us
    psum x2, waiting for transfers between devices: 0.04 us -> 175 us  [shards(): cross, hgram = lax.psum((cross_part, hgram_part), 'tgt')]
    ppermute x0 -> x6, waiting for transfers between devices: none -> 66.2 us  [fill_state(): lax.ppermute(tile_out, axis_name=across, perm=[(pp, pp ^ reply) for pp in...]
    all_gather x1 -> x0, blocking collectives: 47.2 us -> none  [shards(): activation = lax.all_gather(start_w, 'tgt', axis=0, tiled=True)]
    all_to_all x1, waiting for transfers between devices: 43.9 us -> 0.01 us  [shards(): lax.all_to_all(send_weighted, 'tgt', split_axis=0, concat_axis=0, tiled=T...]
    all_to_all x1, waiting for transfers between devices: 17.1 us -> 0.01 us  [shards(): lax.all_to_all(coadd, 'tgt', split_axis=1, concat_axis=0, tiled=True)]
  transfers between devices with their start and end apart: 6 -> 12, of which waited for: 3 -> 7; matrix products, arithmetic and copies ran while one was open for 1% -> 1% of each run, Pallas kernels for 0% -> 0%
where the time goes in v1:
time: 1470 us
  blocking collectives  526 us (36%)
  local copies, waits for them, and re-layouts  333 us (23%)
  waiting for transfers between devices  285 us (19%)
  loops' own time  178 us (12%)
  matrix products  72.3 us (5%)
  starting transfers between devices  49.5 us (3%)
    psum x2, blocking collectives, shards(): cross, hgram = lax.psum((cross_part, hgram_part), 'tgt')  494 us
    psum x2, waiting for transfers between devices, shards(): cross, hgram = lax.psum((cross_part, hgram_part), 'tgt')  175 us
    dynamic_slice x128, local copies, waits for them, and re-layouts, column_step(): wanted = lax.dynamic_index_in_dim(cross, index, 1, keepdims=False)  110 us
    another operation x2, loops' own time, update_columns(): return lax.fori_loop(0, activation.shape[1], column_step, activation)  91.8 us
    another operation x2, loops' own time, update_rows(): return lax.fori_loop(0, templates.shape[0], row_step, templates)  85.8 us
    dynamic_slice x128, local copies, waits for them, and re-layouts, column_step(): pivot = lax.dynamic_index_in_dim(gram_col, index, 0, keepdims=False)  83.7 us
    dynamic_slice x128, local copies, waits for them, and re-layouts, row_step(): pivot = lax.dynamic_index_in_dim(gram_row, index, 0, keepdims=False)  75.3 us
    ppermute x6, waiting for transfers between devices, fill_state(): lax.ppermute(tile_out, axis_name=across, perm=[(pp, pp ^ reply) for pp in...  66.2 us
  transfers between devices with their start and end apart: 12, of which 7 were waited for; matrix products, arithmetic and copies ran while one was open for 1% of the time, Pallas kernels for 0%

profile of v1, /device:TPU:8, one launch (start us, length us, event | category | flops | bytes accessed | tf_op | source)
XLA Modules:
  0.0 1465.5 jit_solution(15227096732878844923)
XLA Ops:
  10.4 1.6 gather_fusion
  13.6 11.9 all-to-all-start
  25.6 6.4 gather_fusion.2
  32.2 3.2 gather_fusion.1
  35.4 4.1 select_multiply_fusion.1
  39.5 1.7 all_to_all.41
  41.2 10.3 all-to-all-start.2
  51.5 5.0 all_to_all.38
  56.6 44.1 %all-to-all-done.2 = bf16[64,2,7808]{2,1,0:T(2,128)(2,1)S(1)} async-done(((bf16[64,2,7808]{2,1,0:T(2,128)(2,1)}), bf16[64,2,7808]{2,1,0:T(2,128)(2,1)S(1)}, u32[]{:S(2)}, u32[]{:S(2)}) %all-to-all-start.2) | async-done | bytes 1998880 | tf_op jit(solution)/shard_map/all_to_all | solution.py:100
  100.6 6.1 all-to-all-start.1
  106.9 1.2 collective-permute-done
  108.1 1.8 collective-permute-start.1
  109.8 42.5 %collective-permute-done.1 = f32[2,32,64]{2,1,0:T(8,128)S(1)} collective-permute-done((f32[2,32,64]{2,1,0:T(8,128)S(1)}, f32[2,32,64]{2,1,0:T(8,128)S(1)}, u32[]{:S(2)}, u32[]{:S(2)}) %collective-permute-start.1) | collective-permute-done | bytes 16416 | tf_op jit(solution)/shard_map/ppermute | solution.py:26
  152.3 1.2 collective-permute-start.2
  153.6 5.0 collective-permute-done.2
  158.6 5.1 collective-permute-start.3
  164.0 6.7 collective-permute-done.3
  170.7 4.3 all_to_all.43
  175.0 1.4 convolution_add_fusion
  176.3 4.3 all_to_all.40
  180.6 1.6 fusion.20
  182.2 2.1 all_to_all.44
  184.3 1.1 copy.23
  185.5 8.1 all-to-all-start.3
  193.7 1.7 collective-permute-start.4
  195.4 10.8 collective-permute-done.4
  206.3 3.0 collective-permute-start.5
  209.5 248.3 %psum.57 = f32[64,64]{1,0:T(8,128)S(1)} all-reduce(f32[64,64]{1,0:T(8,128)S(1)} %fusion.38), channel_id=1, replica_groups=mesh['tgt'=64,'rep'=4] {'tgt'}, use_global_device_ids=true, to_apply=%region_0.1 | all-reduce | flops 4096 | bytes 32768 | tf_op jit(solution)/shard_map/psum | solution.py:117
  457.9 1.1 fusion.30
  459.6 174.8 %all-reduce.5.cloned.1.call-done = f32[2048,64]{0,1:T(8,128)} async-done(((f32[2048,64]{0,1:T(8,128)}), f32[2048,64]{0,1:T(8,128)}) %all-reduce.5.cloned.1.call-update) | async-done | bytes 524304 | tf_op jit(solution)/shard_map/psum | solution.py:117
  634.3 179.7 %while.64 = (s32[]{:T(128)}, f32[2048,64]{0,1:T(8,128)S(1)}, f32[2048,64]{0,1:T(8,128)}, f32[64,64]{0,1:T(8,128)S(1)}, s32[]{:T(128)}, /*index=5*/s32[]{:T(128)}, s32[]{:T(128)}, f32[1,1]{0,1:T(1,128)}) while((s32[]{:T(128)}, f32[2048,64]{0,1:T(8,128)S(1)}, f32[2048,64]{0,1:T(8,128)}, f32[64,64]{0,1:T(8,128)S(1)}, s32[]{:T(128)}, ...), condition=%wide.region_7.9_spmd, body=%wide.region_6.8_spmd.sunk | while | flops 1581060 | bytes 615053 | solution.py:56
  637.1 0.9 constant_dynamic-slice_fusion.20
  640.0 0.9 constant_dynamic-slice_fusion.20
  642.8 0.9 constant_dynamic-slice_fusion.20
  645.6 0.9 constant_dynamic-slice_fusion.20
  648.4 0.9 constant_dynamic-slice_fusion.20
  651.2 0.9 constant_dynamic-slice_fusion.20
  654.0 0.9 constant_dynamic-slice_fusion.20
  656.8 0.9 constant_dynamic-slice_fusion.20
  659.6 0.9 constant_dynamic-slice_fusion.20
  662.4 0.9 constant_dynamic-slice_fusion.20
  665.2 0.9 constant_dynamic-slice_fusion.20
  682.1 0.9 constant_dynamic-slice_fusion.20
  684.9 0.9 constant_dynamic-slice_fusion.20
  687.7 0.9 constant_dynamic-slice_fusion.20
  690.5 0.9 constant_dynamic-slice_fusion.20
  693.3 0.9 constant_dynamic-slice_fusion.20
  696.1 0.9 constant_dynamic-slice_fusion.20
  698.9 0.9 constant_dynamic-slice_fusion.20
  701.7 0.9 constant_dynamic-slice_fusion.20
  707.4 0.9 constant_dynamic-slice_fusion.20
  710.2 0.9 constant_dynamic-slice_fusion.20
  715.8 0.9 constant_dynamic-slice_fusion.20
  718.6 0.9 constant_dynamic-slice_fusion.20
  724.2 0.9 constant_dynamic-slice_fusion.20
  727.0 0.9 constant_dynamic-slice_fusion.20
  729.8 0.9 constant_dynamic-slice_fusion.20
  814.9 14.6 all-reduce.1
  829.5 91.4 %while.65 = (s32[]{:T(128)}, f32[64,122]{1,0:T(8,128)S(1)}, f32[64,122]{1,0:T(8,128)S(1)}, f32[64,64]{1,0:T(8,128)S(1)}, s32[]{:T(128)}, /*index=5*/s32[]{:T(128)}, s32[]{:T(128)}, f32[1,1]{1,0:T(1,128)}) while((s32[]{:T(128)}, f32[64,122]{1,0:T(8,128)S(1)}, f32[64,122]{1,0:T(8,128)S(1)}, f32[64,64]{1,0:T(8,128)S(1)}, s32[]{:T(128)}, ...), condition=%wide.region_11.13_spmd, body=%wide.region_10.12_spmd.sunk | while | flops 94188 | bytes 37433 | solution.py:70
  920.9 1.1 fusion.28
  922.2 246.2 %psum.61 = f32[64,64]{1,0:T(8,128)S(1)} all-reduce(f32[64,64]{1,0:T(8,128)S(1)} %fusion.40), channel_id=1, replica_groups=mesh['tgt'=64,'rep'=4] {'tgt'}, use_global_device_ids=true, to_apply=%region_12.14 | all-reduce | flops 4096 | bytes 32768 | tf_op jit(solution)/shard_map/psum | solution.py:117
  1168.5 179.7 %while.66 = (s32[]{:T(128)}, f32[2048,64]{0,1:T(8,128)S(1)}, f32[2048,64]{0,1:T(8,128)}, f32[64,64]{0,1:T(8,128)S(1)}, s32[]{:T(128)}, /*index=5*/s32[]{:T(128)}, s32[]{:T(128)}, f32[1,1]{0,1:T(1,128)}) while((s32[]{:T(128)}, f32[2048,64]{0,1:T(8,128)S(1)}, f32[2048,64]{0,1:T(8,128)}, f32[64,64]{0,1:T(8,128)S(1)}, s32[]{:T(128)}, ...), condition=%wide.region_15.17_spmd, body=%wide.region_14.16_spmd.sunk | while | flops 1581060 | bytes 615053 | solution.py:56
  1349.3 17.3 %all-reduce = (f32[64,122]{1,0:T(8,128)S(1)}, f32[64,64]{1,0:T(8,128)S(1)}) all-reduce(f32[64,122]{1,0:T(8,128)S(1)} %fusion.21, f32[64,64]{1,0:T(8,128)S(1)} %fusion.41), channel_id=1, replica_groups=mesh['tgt'=64,'rep'=4] {'rep'}, use_global_device_ids=true, to_apply=%region_17.19 | all-reduce | flops 11904 | bytes 95232 | tf_op jit(solution)/shard_map/psum | solution.py:126
  1366.6 91.4 %while.67 = (s32[]{:T(128)}, f32[64,122]{1,0:T(8,128)S(1)}, f32[64,122]{1,0:T(8,128)S(1)}, f32[64,64]{1,0:T(8,128)S(1)}, s32[]{:T(128)}, /*index=5*/s32[]{:T(128)}, s32[]{:T(128)}, f32[1,1]{1,0:T(1,128)}) while((s32[]{:T(128)}, f32[64,122]{1,0:T(8,128)S(1)}, f32[64,122]{1,0:T(8,128)S(1)}, f32[64,64]{1,0:T(8,128)S(1)}, s32[]{:T(128)}, ...), condition=%wide.region_19.21_spmd, body=%wide.region_18.20_spmd.sunk | while | flops 94188 | bytes 37433 | solution.py:70
  (1058 shorter events, 351.6 us)
Async XLA Ops:
  13.6 27.6 %all-to-all-start = ((s32[64,2,1]{1,2,0:T(1,128)}), s32[64,2,1]{1,2,0:T(1,128)S(1)}, u32[]{:S(2)}, u32[]{:S(2)}) async-start(s32[64,2,1]{1,2,0:T(1,128)} %bitcast.45), calls=%async_computation | async-start | bytes 65536 | tf_op jit(solution)/shard_map/all_to_all | solution.py:101
  25.5 6.5 copy-start
  25.5 6.4 copy-start.3
  41.2 59.4 %all-to-all-start.2 = ((bf16[64,2,7808]{2,1,0:T(2,128)(2,1)}), bf16[64,2,7808]{2,1,0:T(2,128)(2,1)S(1)}, u32[]{:S(2)}, u32[]{:S(2)}) async-start(bf16[64,2,7808]{2,1,0:T(2,128)(2,1)} %all_to_all.41), calls=%async_computation.2 | async-start | bytes 3997696 | tf_op jit(solution)/shard_map/all_to_all | solution.py:100
  56.6 50.2 %copy-start.4 = (f32[32,64]{1,0:T(8,128)S(1)}, f32[32,64]{1,0:T(8,128)}, u32[]{:S(2)}) copy-start(f32[32,64]{1,0:T(8,128)} %param.18) | copy-start | bytes 24580
  100.6 6.1 copy-start.2
  100.6 75.7 %all-to-all-start.1 = ((bf16[64,2,7808]{2,1,0:T(2,128)(2,1)}), bf16[64,2,7808]{2,1,0:T(2,128)(2,1)}, u32[]{:S(2)}, u32[]{:S(2)}) async-start(bf16[64,2,7808]{2,1,0:T(2,128)(2,1)} %all_to_all.38), calls=%async_computation.1 | async-start | bytes 3997696 | tf_op jit(solution)/shard_map/all_to_all | solution.py:99
  106.8 1.3 collective-permute-start
  108.1 44.3 %collective-permute-start.1 = (f32[2,32,64]{2,1,0:T(8,128)S(1)}, f32[2,32,64]{2,1,0:T(8,128)S(1)}, u32[]{:S(2)}, u32[]{:S(2)}) collective-permute-start(f32[2,32,64]{2,1,0:T(8,128)S(1)} %get-tuple-element.578), channel_id=1, source_target_pairs={{0,8},{4,12},{8,0},{12,4},{16,24},{20,28},{24,16},{28,20},{32,40},... | collective-permute-start | bytes 49160 | tf_op jit(solution)/shard_map/ppermute | solution.py:26
  152.3 6.2 collective-permute-start.2
  158.6 12.1 collective-permute-start.3
  185.5 272.5 %all-to-all-start.3 = ((bf16[32,64,122]{2,0,1:T(8,128)(2,1)}), bf16[32,64,122]{2,0,1:T(8,128)(2,1)S(1)}, u32[]{:S(2)}, u32[]{:S(2)}) async-start(bf16[32,64,122]{2,0,1:T(8,128)(2,1)} %copy.23), calls=%async_computation.3 | async-start | bytes 1048576 | tf_op jit(solution)/shard_map/all_to_all | solution.py:110
  193.6 440.7 %all-reduce.5.cloned.1.call-start = ((), (), s32[]{:S(2)}) async-start(), calls=%async_computation.4 | async-start | bytes 1048576 | tf_op jit(solution)/shard_map/psum | solution.py:117
  193.7 12.5 collective-permute-start.4
  206.3 251.5 %collective-permute-start.5 = (f32[32,32,64]{2,1,0:T(8,128)S(1)}, f32[32,32,64]{2,1,0:T(8,128)S(1)}, u32[]{:S(2)}, u32[]{:S(2)}) collective-permute-start(f32[32,32,64]{2,1,0:T(8,128)S(1)} %bitcast.166), channel_id=1, source_target_pairs={{0,128},{4,132},{8,136},{12,140},{16,144},{20,148},{24,152},{28,15... | collective-permute-start | bytes 786440 | tf_op jit(solution)/shard_map/ppermute | solution.py:26
  459.1 709.4 %all-reduce.7.cloned.1.call-start = ((), (), s32[]{:S(2)}) async-start(), calls=%async_computation.5 | async-start | bytes 1048576 | tf_op jit(solution)/shard_map/psum | solution.py:117
  1458.0 0.6 copy-start.1
Sparse Core Ops, SparseCore 0:
  459.2 175.1 all-reduce.4
  922.1 180.2 all-reduce.6
